TPU v7x, 32 devices: a whole 2x2x4 slice. The times are simulated.
32 devices in a mesh: groups: 2 (over x), lat: 16 (over z, y, core).
Axes of the slice: x: 2, y: 2, z: 4, core: 2. Of those that a mesh axis runs over, the one named last changes fastest.
Arguments:
- grid_latent: bfloat16 [16384, 512], P(('groups', 'lat')), parts along dimension 0, may hold values from -6 to 6
- mesh_latent: bfloat16 [16384, 512], P(('groups', 'lat')), parts along dimension 0, may hold values from -6 to 6
- g2m_edge: bfloat16 [48, 512, 512], P('lat'), may hold values from -6 to 6
- g2m_sender: int32 [48, 512], P('lat'), may hold values from 0 to 511
- g2m_receiver: int32 [48, 512], P('lat'), may hold values from 0 to 512, as said below
- fine_edge: bfloat16 [16384, 512], P('lat'), may hold values from -6 to 6
- fine_sender: int32 [16384], P('lat'), may hold values from 0 to 575
- fine_receiver: int32 [16384], P('lat'), may hold values from 0 to 511
- coarse_edge: bfloat16 [256, 8, 512], P('lat'), may hold values from -6 to 6
- coarse_sender: int32 [256, 8], P('lat'), may hold values from 0 to 511
- coarse_receiver: int32 [256, 8], P('lat'), may hold values from 0 to 512, as said below
- enc_edge_in: bfloat16 [1536, 512], replicated, may hold values from -0.15625 to 0.15625
- enc_edge_out: bfloat16 [512, 512], replicated, may hold values from -0.25 to 0.25
- enc_edge_par: float32 [3, 512], replicated, may hold values from -1.5 to 1.5
- enc_node_in: bfloat16 [1024, 512], replicated, may hold values from -0.1875 to 0.1875
- enc_node_out: bfloat16 [512, 512], replicated, may hold values from -0.25 to 0.25
- enc_node_par: float32 [3, 512], replicated, may hold values from -1.5 to 1.5
- proc_edge_in: bfloat16 [1536, 512], replicated, may hold values from -0.15625 to 0.15625
- proc_edge_out: bfloat16 [512, 512], replicated, may hold values from -0.25 to 0.25
- proc_edge_par: float32 [3, 512], replicated, may hold values from -1.5 to 1.5
- proc_node_in: bfloat16 [1024, 512], replicated, may hold values from -0.1875 to 0.1875
- proc_node_out: bfloat16 [512, 512], replicated, may hold values from -0.25 to 0.25
- proc_node_par: float32 [3, 512], replicated, may hold values from -1.5 to 1.5
Outputs:
- mesh_out: bfloat16 [16384, 512], P(('groups', 'lat')), parts along dimension 0
There are 2 independent parts, one for each index of `groups`. A program takes and returns all parts, laid end to end along the dimension named above; an argument that names none is the same for every part. Nothing has to cross between parts.
Inputs may be any that keep to these rules, and one draw needn't show every extreme that they name: `g2m_receiver`: the value 512 marks an empty slot; rows whose source device d - j + 1 lies outside 0 to 15 are empty. `coarse_receiver`: entries for a receiving device d lie in rows d * 16 to d * 16 + 15; the value 512 marks an empty slot; pairs of devices more than 8 apart have only empty slots.
All inputs are finite; a program needn't handle non-finite values.
Results may differ from a plain program's by a relative error of at most 0.007.
Values may be sent and summed in bfloat16 or wider, within the bound.
A program may use at most 128 MiB of HBM per device.

v0:
```python
import jax
import jax.numpy as jnp
from jax import lax
from jax.sharding import PartitionSpec as P

BR = 32


def padded(block, sides, width):
    for axis, dim in sides:
        count = lax.axis_size(axis)
        forward = [(i, i + 1) for i in range(count - 1)]
        backward = [(target, source) for source, target in forward]
        low = lax.ppermute(
            lax.slice_in_dim(block, block.shape[dim] - width, None, axis=dim), axis, forward
        )
        high = lax.ppermute(lax.slice_in_dim(block, 0, width, axis=dim), axis, backward)
        block = jnp.concatenate([low, block, high], axis=dim)
    return block


def layer_norm(values, params):
    average = jnp.mean(values, axis=-1, keepdims=True)
    centred = values - average
    spread = jnp.mean(centred * centred, axis=-1, keepdims=True)
    return centred * lax.rsqrt(spread + 1e-05) * params[1] + params[2]


def edge_message(preact, w_out, params):
    hidden = jax.nn.silu(preact + params[0]).astype(jnp.bfloat16)
    output = jnp.dot(hidden, w_out, preferred_element_type=jnp.float32)
    return layer_norm(output, params).astype(jnp.bfloat16)


def node_update(latent, summed, w_in, w_out, params):
    breadth = latent.shape[1]
    preact = jnp.dot(latent, w_in[:breadth], preferred_element_type=jnp.float32)
    preact = preact + jnp.dot(
        summed.astype(jnp.bfloat16), w_in[breadth:], preferred_element_type=jnp.float32
    )
    hidden = jax.nn.silu(preact + params[0]).astype(jnp.bfloat16)
    output = layer_norm(jnp.dot(hidden, w_out, preferred_element_type=jnp.float32), params)
    return (latent.astype(jnp.float32) + output).astype(jnp.bfloat16)


def one_hot(indices, extent):
    columns = lax.broadcasted_iota(jnp.int32, (indices.shape[0], extent), 1)
    return (indices[:, None] == columns).astype(jnp.bfloat16)


def sum_rows(selector, message):
    return lax.dot_general(
        selector, message, (((0,), (0,)), ((), ())), preferred_element_type=jnp.float32
    )


def project_pair(edge_rows, grid_rows, w_edge, w_send):
    breadth = edge_rows.shape[-1]
    total = jnp.dot(edge_rows.reshape(-1, breadth), w_edge, preferred_element_type=jnp.float32)
    total = total + jnp.dot(
        grid_rows.reshape(-1, breadth), w_send, preferred_element_type=jnp.float32
    )
    return total.astype(jnp.bfloat16).reshape(edge_rows.shape)


def incoming_rows(extended):
    return jnp.stack([extended[4], extended[2], extended[0]], axis=0)


def per_device(
    grid_latent,
    mesh_latent,
    g2m_edge,
    g2m_sender,
    g2m_receiver,
    fine_edge,
    fine_sender,
    fine_receiver,
    coarse_edge,
    coarse_sender,
    coarse_receiver,
    enc_edge_in,
    enc_edge_out,
    enc_edge_par,
    enc_node_in,
    enc_node_out,
    enc_node_par,
    proc_edge_in,
    proc_edge_out,
    proc_edge_par,
    proc_node_in,
    proc_node_out,
    proc_node_par,
):
    breadth = mesh_latent.shape[1]
    mesh_count = mesh_latent.shape[0]
    grid_rows = grid_latent[g2m_sender]
    stacked = jnp.stack([g2m_edge, grid_rows], axis=1)
    extended_in = padded(stacked, (("lat", 0),), 1)
    chosen = incoming_rows(extended_in)
    arrived = project_pair(
        chosen[:, 0], chosen[:, 1], enc_edge_in[:breadth], enc_edge_in[breadth : 2 * breadth]
    )
    selector = one_hot(g2m_receiver.reshape(-1), mesh_count)
    recv_table = jnp.dot(
        mesh_latent, enc_edge_in[2 * breadth :], preferred_element_type=jnp.float32
    ).astype(jnp.bfloat16)
    preact = arrived.reshape(-1, breadth).astype(jnp.float32) + jnp.dot(
        selector, recv_table, preferred_element_type=jnp.float32
    )
    message = edge_message(preact, enc_edge_out, enc_edge_par)
    mesh_enc = node_update(
        mesh_latent, sum_rows(selector, message), enc_node_in, enc_node_out, enc_node_par
    )
    proc_send = proc_edge_in[breadth : 2 * breadth]
    payload = jnp.dot(mesh_enc, proc_send, preferred_element_type=jnp.float32).astype(jnp.bfloat16)
    extended = padded(payload, (("lat", 0),), BR)
    far_rows = lax.all_to_all(
        payload[coarse_sender], "lat", split_axis=0, concat_axis=0, tiled=True
    ).reshape(-1, breadth)
    near_terms = jnp.dot(
        one_hot(fine_sender, extended.shape[0]), extended, preferred_element_type=jnp.float32
    )
    send_terms = jnp.concatenate([near_terms, far_rows.astype(jnp.float32)], axis=0)
    receivers_all = jnp.concatenate([fine_receiver, coarse_receiver.reshape(-1)], axis=0)
    selector_all = one_hot(receivers_all, mesh_count)
    recv_proj = jnp.dot(
        mesh_enc, proc_edge_in[2 * breadth :], preferred_element_type=jnp.float32
    ).astype(jnp.bfloat16)
    edge_all = jnp.concatenate([fine_edge, coarse_edge.reshape(-1, breadth)], axis=0)
    preact = (
        jnp.dot(edge_all, proc_edge_in[:breadth], preferred_element_type=jnp.float32) + send_terms
    )
    preact = preact + jnp.dot(selector_all, recv_proj, preferred_element_type=jnp.float32)
    message = edge_message(preact, proc_edge_out, proc_edge_par)
    return node_update(
        mesh_enc, sum_rows(selector_all, message), proc_node_in, proc_node_out, proc_node_par
    )


def solution(mesh):
    in_specs = (
        P(("groups", "lat"), None),
        P(("groups", "lat"), None),
        P("lat", None, None),
        P("lat", None),
        P("lat", None),
        P("lat", None),
        P("lat"),
        P("lat"),
        P("lat", None, None),
        P("lat", None),
        P("lat", None),
        P(),
        P(),
        P(),
        P(),
        P(),
        P(),
        P(),
        P(),
        P(),
        P(),
        P(),
        P(),
    )
    out_specs = P(("groups", "lat"), None)
    return jax.shard_map(
        per_device, mesh=mesh, in_specs=in_specs, out_specs=out_specs, check_vma=False
    )
```

profile of v0, /device:TPU:0, one launch (start us, length us, event | category | flops | bytes accessed | tf_op | source)
XLA Modules:
  0.0 90.1 jit_solution(13833511106981887444)
XLA Ops:
  0.0 0.0 copy-start
  0.0 0.8 compare_select_fusion
  0.8 6.0 %gather_fusion = bf16[1536,512]{1,0:T(8,128)(2,1)S(1)} fusion(bf16[512,512]{1,0:T(8,128)(2,1)} %param.23, s32[2048]{0:T(1024)S(1)} %pad_clamp_fusion), kind=kCustom, calls=%fused_computation | custom fusion | bytes 3151872 | tf_op jit(solution)/shard_map/gather | solution.py:97
  6.8 0.0 copy-start.6
  6.8 0.0 copy-start.5
  6.8 0.0 copy-start.7
  6.8 0.0 copy-start.12
  6.8 0.0 copy-start.8
  6.8 0.0 copy-start.10
  6.8 0.0 copy-start.11
  6.8 0.0 copy-start.9
  6.9 3.0 %fusion.37 = (bf16[1,2,512,512]{3,2,0,1:T(8,128)(2,1)}, bf16[1,2,512,512]{3,2,0,1:T(8,128)(2,1)}, bf16[1,2,512,512]{3,2,0,1:T(8,128)(2,1)S(1)}) fusion(bf16[3,1,512,512]{3,2,0,1:T(8,128)(2,1)} %bitcast.39, bf16[3,1,512,512]{3,2,0,1:T(8,128)(2,1)S(1)} %bitcast.37), kind=kLoop, calls=%fused_computation.58 | loop fusion | flops 1572864 | bytes 6291456 | tf_op jit(solution)/shard_map/stack | solution.py:98
  9.8 1.4 %collective-permute-start = (bf16[1,2,512,512]{3,2,0,1:T(8,128)(2,1)}, bf16[1,2,512,512]{3,2,0,1:T(8,128)(2,1)}, u32[]{:S(2)}, u32[]{:S(2)}) collective-permute-start(bf16[1,2,512,512]{3,2,0,1:T(8,128)(2,1)} %get-tuple-element.7), channel_id=1, source_target_pairs={{1,0},{2,1},{3,2},{4,3},{5,4},{6,5},{7,6},{8,7},{9,8},{10,9},{11,1... | collective-permute-start | bytes 3145736 | tf_op jit(solution)/shard_map/ppermute | solution.py:17
  11.3 4.0 %collective-permute-start.1 = (bf16[1,2,512,512]{3,2,0,1:T(8,128)(2,1)}, bf16[1,2,512,512]{3,2,0,1:T(8,128)(2,1)}, u32[]{:S(2)}, u32[]{:S(2)}) collective-permute-start(bf16[1,2,512,512]{3,2,0,1:T(8,128)(2,1)} %get-tuple-element.8), channel_id=1, source_target_pairs={{0,1},{1,2},{2,3},{3,4},{4,5},{5,6},{6,7},{7,8},{8,9},{9,10},{10,1... | collective-permute-start | bytes 3145736 | tf_op jit(solution)/shard_map/ppermute | solution.py:14
  15.3 0.0 copy-done.6
  15.3 0.0 copy-done.5
  15.4 0.0 copy-start.15
  15.4 1.3 %copy.28 = bf16[512,512]{0,1:T(8,128)(2,1)S(1)} copy(bf16[512,512]{1,0:T(8,128)(2,1)} %param.24) | data formatting | bytes 1048576 | tf_op args[1]
  16.7 0.0 copy-done.12
  16.7 0.1 copy.30
  16.8 0.1 reshape.73
  16.9 0.1 copy.29
  17.0 0.1 reshape.60
  17.1 0.0 copy-start.13
  17.1 2.5 %convolution_convert_fusion.2 = bf16[512,512]{1,0:T(8,128)(2,1)} fusion(bf16[512,512]{1,0:T(8,128)(2,1)} %param.24, bf16[1536,512]{1,0:T(8,128)(2,1)} %param.34), kind=kOutput, calls=%fused_computation.42 | convolution fusion | flops 268697600 | bytes 1572864 | tf_op jit(solution)/shard_map/dot_general | solution.py:105
  19.6 2.5 %fusion.62 = f32[512,512]{1,0:T(8,128)} fusion(bf16[512,512]{1,0:T(8,128)(2,1)S(1)} %copy-done.2, bf16[1024,512]{1,0:T(8,128)(2,1)} %param.37), kind=kOutput, calls=%fused_computation.88 | convolution fusion | flops 268435456 | bytes 2097152 | tf_op jit(solution)/shard_map/dot_general | solution.py:37
  22.1 0.0 copy-done.15
  22.1 3.3 %fusion.23 = f32[1152,512]{1,0:T(8,128)} fusion(bf16[128,512]{1,0:T(8,128)(2,1)S(1)} %bitcast.52, bf16[1024,512]{1,0:T(8,128)(2,1)S(1)} %copy-done.13, bf16[1536,512]{1,0:T(8,128)(2,1)} %param.40), kind=kOutput, calls=%fused_computation.45 | convolution fusion | flops 606339072 | bytes 4063232 | tf_op jit(solution)/shard_map/dot_general | solution.py:132
  25.4 0.0 collective-permute-done
  25.4 0.0 collective-permute-done.1
  25.4 1.9 %pad_maximum_fusion = bf16[3,2,512,512]{3,2,0,1:T(8,128)(2,1)S(1)} fusion(bf16[1,2,512,512]{3,2,0,1:T(8,128)(2,1)} %collective-permute-done.1, bf16[1,2,512,512]{3,2,0,1:T(8,128)(2,1)S(1)} %get-tuple-element.9, bf16[1,2,512,512]{3,2,0,1:T(8,128)(2,1)} %collective-permute-done), kind=kLoop, calls=%fused_computation.11 | loop fusion | flops 3145728 | bytes 6291456 | tf_op jit(solution)/shard_map/stack | solution.py:67
  27.3 0.0 copy-start.3
  27.3 0.2 fusion.71
  27.5 1.2 %copy-done.3 = bf16[1536,512]{1,0:T(8,128)(2,1)S(1)} copy-done((bf16[1536,512]{1,0:T(8,128)(2,1)S(1)}, bf16[1536,512]{1,0:T(8,128)(2,1)}, u32[]{:S(2)}) %copy-start.3) | copy-done | bytes 1572888
  28.7 1.0 %fusion.59 = f32[1536,512]{1,0:T(8,128)S(1)} fusion(bf16[1536,512]{1,0:T(8,128)(2,1)S(1)} %bitcast.36, bf16[1536,512]{1,0:T(8,128)(2,1)S(1)} %copy-done.3), kind=kOutput, calls=%fused_computation.85 | convolution fusion | flops 805306368 | bytes 5242880 | tf_op jit(solution)/shard_map/dot_general | solution.py:60
  29.7 0.0 copy-start.17
  29.7 1.0 %fusion.3 = bf16[1536,512]{1,0:T(8,128)(2,1)S(1)} fusion(f32[1536,512]{1,0:T(8,128)S(1)} %fusion.59, bf16[1536,512]{1,0:T(8,128)(2,1)S(1)} %bitcast.38, bf16[1536,512]{1,0:T(8,128)(2,1)S(1)} %copy-done.3), kind=kOutput, calls=%fused_computation.17 | convolution fusion | flops 806879232 | bytes 6815744 | tf_op jit(solution)/shard_map/dot_general | solution.py:59
  30.8 4.0 %fusion.77 = (f32[1536]{0:T(1024)S(1)}, f32[1536,512]{0,1:T(8,128)}) fusion(bf16[512,512]{1,0:T(8,128)(2,1)S(1)} %copy-done, bf16[512,512]{1,0:T(8,128)(2,1)S(1)} %copy-done.17, bf16[1536,512]{1,0:T(8,128)(2,1)S(1)} %fusion.3, f32[512]{0:T(512)S(1)} %bitcast.51, s32[1536]{0:T(1024)S(1)} %eq.26), kind=kOutput, calls=%fused_computation.117 | convolution fusion | flops 1618475520 | bytes 5781504 | tf_op jit(solution)/shard_map/dot_general | solution.py:31
  34.7 2.4 %multiply_reduce_fusion = f32[1536]{0:T(1024)S(1)} fusion(f32[1536,512]{0,1:T(8,128)} %get-tuple-element.25, f32[1536]{0:T(1024)S(1)} %broadcast_multiply_fusion.1), kind=kLoop, calls=%fused_computation.13 | loop fusion | flops 2357760 | bytes 3158016 | tf_op jit(solution)/shard_map/reduce_sum | solution.py:25
  37.1 0.4 copy-done.1
  37.6 1.5 %fusion.19 = bf16[512,512]{1,0:T(8,128)(2,1)S(1)} fusion(f32[1536,512]{0,1:T(8,128)S(1)} %copy-done.1, f32[512]{0:T(512)S(1)} %bitcast.50, f32[512]{0:T(512)S(1)} %bitcast.49, f32[1536]{0:T(1024)S(1)} %add_rsqrt_fusion.1, f32[1536]{0:T(1024)S(1)} %broadcast_multiply_fusion.1, s32[1536]{0:T(1024)S(1)} %eq.26), kind=kOutput, calls=%fused_computation.44 | convolution fusion | flops 811073536 | bytes 3692544 | tf_op jit(solution)/shard_map/dot_general | solution.py:52
  39.1 2.4 %fusion.78 = (f32[512]{0:T(512)S(1)}, f32[512,512]{0,1:T(8,128)S(1)}) fusion(bf16[512,512]{1,0:T(8,128)(2,1)S(1)} %copy-done.14, f32[512,512]{1,0:T(8,128)} %fusion.62, bf16[512,512]{1,0:T(8,128)(2,1)S(1)} %fusion.19, f32[512]{0:T(512)S(1)} %bitcast.48, bf16[1024,512]{1,0:T(8,128)(2,1)} %param.37), kind=kOutput, calls=%fused_computation.118 | convolution fusion | flops 538967552 | bytes 3674112 | tf_op jit(solution)/shard_map/dot_general | solution.py:42
  41.5 0.2 multiply_reduce_fusion.3
  41.7 0.3 add_convert_fusion.7
  42.0 0.0 copy-start.4
  42.0 1.6 %convolution_convert_fusion.1 = bf16[512,512]{1,0:T(8,128)(2,1)S(1)} fusion(bf16[512,512]{0,1:T(8,128)(2,1)S(1)} %add_convert_fusion.7, bf16[1536,512]{1,0:T(8,128)(2,1)} %param.40), kind=kOutput, calls=%fused_computation.41 | convolution fusion | flops 268697600 | bytes 1572864 | tf_op jit(solution)/shard_map/dot_general | solution.py:116
  43.7 15.7 %collective-permute-start.2 = (bf16[32,512]{1,0:T(8,128)(2,1)S(1)}, bf16[32,512]{1,0:T(8,128)(2,1)S(1)}, u32[]{:S(2)}, u32[]{:S(2)}) collective-permute-start(bf16[32,512]{1,0:T(8,128)(2,1)S(1)} %get-tuple-element.10), channel_id=1, source_target_pairs={{0,1},{1,2},{2,3},{3,4},{4,5},{5,6},{6,7},{7,8},{8,9},{9,10},{10,1... | collective-permute-start | bytes 98312 | tf_op jit(solution)/shard_map/ppermute | solution.py:14
  59.3 1.3 %collective-permute-start.3 = (bf16[32,512]{1,0:T(8,128)(2,1)S(1)}, bf16[32,512]{1,0:T(8,128)(2,1)S(1)}, u32[]{:S(2)}, u32[]{:S(2)}) collective-permute-start(bf16[32,512]{1,0:T(8,128)(2,1)S(1)} %get-tuple-element.11), channel_id=1, source_target_pairs={{1,0},{2,1},{3,2},{4,3},{5,4},{6,5},{7,6},{8,7},{9,8},{10,9},{11,1... | collective-permute-start | bytes 98312 | tf_op jit(solution)/shard_map/ppermute | solution.py:17
  60.6 1.5 %gather_fusion.1 = bf16[128,512]{1,0:T(8,128)(2,1)} fusion(bf16[512,512]{1,0:T(8,128)(2,1)S(1)} %convolution_convert_fusion.1, s32[1024]{0:T(1024)S(1)} %pad_clamp_fusion.1), kind=kCustom, calls=%fused_computation.1 | custom fusion | bytes 262656 | tf_op jit(solution)/shard_map/gather | solution.py:119
  62.1 8.3 %all-to-all-start = ((bf16[16,8,512]{2,1,0:T(8,128)(2,1)}), bf16[16,8,512]{2,1,0:T(8,128)(2,1)S(1)}, u32[]{:S(2)}, u32[]{:S(2)}) async-start(bf16[16,8,512]{2,1,0:T(8,128)(2,1)} %bitcast.11), calls=%async_computation | async-start | bytes 262144 | tf_op jit(solution)/shard_map/all_to_all | solution.py:118
  70.4 1.4 %fusion.51 = f32[512,512]{1,0:T(8,128)} fusion(bf16[512,512]{0,1:T(8,128)(2,1)S(1)} %add_convert_fusion.7, bf16[1024,512]{1,0:T(8,128)(2,1)S(1)} %copy-done.4), kind=kOutput, calls=%fused_computation.78 | convolution fusion | flops 268435456 | bytes 2097152 | tf_op jit(solution)/shard_map/dot_general | solution.py:37
  71.9 2.3 %convolution_convert_fusion = bf16[512,512]{1,0:T(8,128)(2,1)} fusion(bf16[512,512]{0,1:T(8,128)(2,1)S(1)} %add_convert_fusion.7, bf16[1536,512]{1,0:T(8,128)(2,1)} %param.40), kind=kOutput, calls=%fused_computation.40 | convolution fusion | flops 268697600 | bytes 1572864 | tf_op jit(solution)/shard_map/dot_general | solution.py:127
  74.2 0.0 collective-permute-done.2
  74.2 0.0 collective-permute-done.3
  74.2 2.4 %fusion.4 = f32[1024,512]{1,0:T(8,128)} fusion(s32[1024]{0:T(1024)S(1)} %copy-done.16, bf16[32,512]{1,0:T(8,128)(2,1)S(1)} %collective-permute-done.3, bf16[512,512]{1,0:T(8,128)(2,1)S(1)} %convolution_convert_fusion.1, bf16[32,512]{1,0:T(8,128)(2,1)S(1)} %collective-permute-done.2), kind=kOutput, calls=%fused_computation.19 | convolution fusion | flops 606339072 | bytes 2691072 | tf_op jit(solution)/shard_map/dot_general | solution.py:121
  76.5 1.8 %all-to-all-done = bf16[16,8,512]{2,1,0:T(8,128)(2,1)S(1)} async-done(((bf16[16,8,512]{2,1,0:T(8,128)(2,1)}), bf16[16,8,512]{2,1,0:T(8,128)(2,1)S(1)}, u32[]{:S(2)}, u32[]{:S(2)}) %all-to-all-start) | async-done | bytes 131104 | tf_op jit(solution)/shard_map/all_to_all | solution.py:118
  78.3 0.7 bitcast_convert_fusion
  79.1 4.4 %fusion.81 = (f32[1152]{0:T(1024)S(1)}, f32[1152,512]{0,1:T(8,128)S(1)}) fusion(bf16[512,512]{1,0:T(8,128)(2,1)} %param.41, bf16[512,512]{1,0:T(8,128)(2,1)} %convolution_convert_fusion, f32[1152,512]{1,0:T(8,128)} %fusion.23, f32[128,512]{1,0:T(8,128)} %bitcast_convert_fusion, f32[1024,512]{1,0:T(8,128)} %fusion.4, f32[512]{0:T(512)S(1)} %bitcast.47, ...), kind=kOutput, calls=%fused_computation.119 | convolution fusion | flops 1214446464 | bytes 8137728 | tf_op jit(solution)/shard_map/dot_general | solution.py:31
  83.5 0.3 multiply_reduce_fusion.1
  83.7 2.1 %convolution_convert_fusion.3 = bf16[512,512]{1,0:T(8,128)(2,1)} fusion(f32[1152,512]{0,1:T(8,128)S(1)} %get-tuple-element.29, f32[512]{0:T(512)S(1)} %bitcast.46, f32[512]{0:T(512)S(1)} %bitcast.45, f32[1152]{0:T(1024)S(1)} %add_rsqrt_fusion, f32[1152]{0:T(1024)S(1)} %broadcast_multiply_fusion, s32[1152]{0:T(1024)S(1)} %pad_add_fusion), kind=kOutput, calls=%fused_computation.43 | convolution fusion | flops 608370688 | bytes 2901504 | tf_op jit(solution)/shard_map/dot_general | solution.py:52
  85.9 2.7 %fusion.82 = (f32[512]{0:T(512)S(1)}, f32[512,512]{0,1:T(8,128)S(1)}) fusion(bf16[512,512]{1,0:T(8,128)(2,1)} %param.44, f32[512,512]{1,0:T(8,128)} %fusion.51, bf16[512,512]{1,0:T(8,128)(2,1)} %convolution_convert_fusion.3, f32[512]{0:T(512)S(1)} %bitcast.44, bf16[1024,512]{1,0:T(8,128)(2,1)} %param.43), kind=kOutput, calls=%fused_computation.120 | convolution fusion | flops 538967552 | bytes 3674112 | tf_op jit(solution)/shard_map/dot_general | solution.py:42
  88.6 0.2 multiply_reduce_fusion.2
  88.7 0.3 add_convert_fusion.6
  89.0 1.0 %copy.31 = bf16[512,512]{1,0:T(8,128)(2,1)} copy(bf16[512,512]{0,1:T(8,128)(2,1)S(1)} %add_convert_fusion.6) | data formatting | bytes 1048576 | tf_op jit(solution)/shard_map/convert_element_type | solution.py:43
  (35 shorter events, 0.2 us)
Async XLA Ops:
  0.0 30.7 %copy-start = (bf16[512,512]{1,0:T(8,128)(2,1)S(1)}, bf16[512,512]{1,0:T(8,128)(2,1)}, u32[]{:S(2)}) copy-start(bf16[512,512]{1,0:T(8,128)(2,1)} %param.35) | copy-start | bytes 1572868
  6.8 8.5 %copy-start.6 = (f32[3,512]{1,0:T(4,128)S(1)}, f32[3,512]{1,0:T(4,128)}, u32[]{:S(2)}) copy-start(f32[3,512]{1,0:T(4,128)} %param.36) | copy-start | bytes 18436
  6.8 8.5 %copy-start.5 = (s32[3,512]{1,0:T(4,128)S(1)}, s32[3,512]{1,0:T(4,128)}, u32[]{:S(2)}) copy-start(s32[3,512]{1,0:T(4,128)} %param.27) | copy-start | bytes 18436
  6.8 8.6 %copy-start.7 = (f32[3,512]{1,0:T(4,128)S(1)}, f32[3,512]{1,0:T(4,128)}, u32[]{:S(2)}) copy-start(f32[3,512]{1,0:T(4,128)} %param.39) | copy-start | bytes 18436
  6.8 9.9 %copy-start.12 = (s32[16,8]{0,1:T(8,128)S(1)}, s32[16,8]{0,1:T(8,128)}, u32[]{:S(2)}) copy-start(s32[16,8]{0,1:T(8,128)} %param.32) | copy-start | bytes 1540
  6.8 10.1 %copy-start.8 = (f32[3,512]{1,0:T(4,128)S(1)}, f32[3,512]{1,0:T(4,128)}, u32[]{:S(2)}) copy-start(f32[3,512]{1,0:T(4,128)} %param.42) | copy-start | bytes 18436
  6.8 10.1 %copy-start.10 = (s32[16,8]{0,1:T(8,128)S(1)}, s32[16,8]{0,1:T(8,128)}, u32[]{:S(2)}) copy-start(s32[16,8]{0,1:T(8,128)} %param.33) | copy-start | bytes 1540
  6.8 10.2 %copy-start.11 = (s32[1024]{0:T(1024)S(1)}, s32[1024]{0:T(1024)}, u32[]{:S(2)}) copy-start(s32[1024]{0:T(1024)} %param.30) | copy-start | bytes 12292
  6.8 10.2 %copy-start.9 = (f32[3,512]{1,0:T(4,128)S(1)}, f32[3,512]{1,0:T(4,128)}, u32[]{:S(2)}) copy-start(f32[3,512]{1,0:T(4,128)} %param.45) | copy-start | bytes 18436
  9.8 9.8 %copy-start.2 = (bf16[512,512]{1,0:T(8,128)(2,1)S(1)}, bf16[512,512]{1,0:T(8,128)(2,1)}, u32[]{:S(2)}) copy-start(bf16[512,512]{1,0:T(8,128)(2,1)} %param.24) | copy-start | bytes 1572868
  9.8 15.5 %collective-permute-start = (bf16[1,2,512,512]{3,2,0,1:T(8,128)(2,1)}, bf16[1,2,512,512]{3,2,0,1:T(8,128)(2,1)}, u32[]{:S(2)}, u32[]{:S(2)}) collective-permute-start(bf16[1,2,512,512]{3,2,0,1:T(8,128)(2,1)} %get-tuple-element.7), channel_id=1, source_target_pairs={{1,0},{2,1},{3,2},{4,3},{5,4},{6,5},{7,6},{8,7},{9,8},{10,9},{11,1... | collective-permute-start | bytes 3145736 | tf_op jit(solution)/shard_map/ppermute | solution.py:17
  11.3 14.1 %collective-permute-start.1 = (bf16[1,2,512,512]{3,2,0,1:T(8,128)(2,1)}, bf16[1,2,512,512]{3,2,0,1:T(8,128)(2,1)}, u32[]{:S(2)}, u32[]{:S(2)}) collective-permute-start(bf16[1,2,512,512]{3,2,0,1:T(8,128)(2,1)} %get-tuple-element.8), channel_id=1, source_target_pairs={{0,1},{1,2},{2,3},{3,4},{4,5},{5,6},{6,7},{7,8},{8,9},{9,10},{10,1... | collective-permute-start | bytes 3145736 | tf_op jit(solution)/shard_map/ppermute | solution.py:14
  15.4 6.7 %copy-start.15 = (bf16[16,8,512]{2,1,0:T(8,128)(2,1)S(1)}, bf16[16,8,512]{2,1,0:T(8,128)(2,1)}, u32[]{:S(2)}) copy-start(bf16[16,8,512]{2,1,0:T(8,128)(2,1)} %param.31) | copy-start | bytes 393220
  17.1 5.0 %copy-start.13 = (bf16[1024,512]{1,0:T(8,128)(2,1)S(1)}, bf16[1024,512]{1,0:T(8,128)(2,1)}, u32[]{:S(2)}) copy-start(bf16[1024,512]{1,0:T(8,128)(2,1)} %param.28) | copy-start | bytes 3145732
  27.3 1.4 %copy-start.3 = (bf16[1536,512]{1,0:T(8,128)(2,1)S(1)}, bf16[1536,512]{1,0:T(8,128)(2,1)}, u32[]{:S(2)}) copy-start(bf16[1536,512]{1,0:T(8,128)(2,1)} %param.34) | copy-start | bytes 4718596
  29.7 1.1 %copy-start.17 = (bf16[512,512]{1,0:T(8,128)(2,1)S(1)}, bf16[512,512]{1,0:T(8,128)(2,1)}, u32[]{:S(2)}) copy-start(bf16[512,512]{1,0:T(8,128)(2,1)} %convolution_convert_fusion.2) | copy-start | bytes 1572868
  34.7 2.8 %copy-start.1 = (f32[1536,512]{0,1:T(8,128)S(1)}, f32[1536,512]{0,1:T(8,128)}, u32[]{:S(2)}) copy-start(f32[1536,512]{0,1:T(8,128)} %get-tuple-element.25) | copy-start | bytes 9437188
  37.6 1.6 %copy-start.14 = (bf16[512,512]{1,0:T(8,128)(2,1)S(1)}, bf16[512,512]{1,0:T(8,128)(2,1)}, u32[]{:S(2)}) copy-start(bf16[512,512]{1,0:T(8,128)(2,1)} %param.38) | copy-start | bytes 1572868
  42.0 28.4 %copy-start.4 = (bf16[1024,512]{1,0:T(8,128)(2,1)S(1)}, bf16[1024,512]{1,0:T(8,128)(2,1)}, u32[]{:S(2)}) copy-start(bf16[1024,512]{1,0:T(8,128)(2,1)} %param.43) | copy-start | bytes 3145732
  43.7 30.5 %collective-permute-start.2 = (bf16[32,512]{1,0:T(8,128)(2,1)S(1)}, bf16[32,512]{1,0:T(8,128)(2,1)S(1)}, u32[]{:S(2)}, u32[]{:S(2)}) collective-permute-start(bf16[32,512]{1,0:T(8,128)(2,1)S(1)} %get-tuple-element.10), channel_id=1, source_target_pairs={{0,1},{1,2},{2,3},{3,4},{4,5},{5,6},{6,7},{7,8},{8,9},{9,10},{10,1... | collective-permute-start | bytes 98312 | tf_op jit(solution)/shard_map/ppermute | solution.py:14
  59.3 14.8 %collective-permute-start.3 = (bf16[32,512]{1,0:T(8,128)(2,1)S(1)}, bf16[32,512]{1,0:T(8,128)(2,1)S(1)}, u32[]{:S(2)}, u32[]{:S(2)}) collective-permute-start(bf16[32,512]{1,0:T(8,128)(2,1)S(1)} %get-tuple-element.11), channel_id=1, source_target_pairs={{1,0},{2,1},{3,2},{4,3},{5,4},{6,5},{7,6},{8,7},{9,8},{10,9},{11,1... | collective-permute-start | bytes 98312 | tf_op jit(solution)/shard_map/ppermute | solution.py:17
  62.1 12.1 %copy-start.16 = (s32[1024]{0:T(1024)S(1)}, s32[1024]{0:T(1024)}, u32[]{:S(2)}) copy-start(s32[1024]{0:T(1024)} %param.29) | copy-start | bytes 12292
  62.1 16.2 %all-to-all-start = ((bf16[16,8,512]{2,1,0:T(8,128)(2,1)}), bf16[16,8,512]{2,1,0:T(8,128)(2,1)S(1)}, u32[]{:S(2)}, u32[]{:S(2)}) async-start(bf16[16,8,512]{2,1,0:T(8,128)(2,1)} %bitcast.11), calls=%async_computation | async-start | bytes 262144 | tf_op jit(solution)/shard_map/all_to_all | solution.py:118
where the time goes:
time: 90.8 us; the launch traced here: 90.1 us
  matrix products  35.1 us (39%)
  starting transfers between devices  30.7 us (34%)
  local copies, waits for them, and re-layouts  12.1 us (13%)
  other arithmetic  10 us (11%)
  waiting for transfers between devices  1.81 us (2%)
    ppermute x2, starting transfers between devices, padded(): lax.ppermute(lax.slice_in_dim(block, block.shape[dim] - width, None, axis...  19.7 us
    dot_general x2, matrix products, edge_message(): output = jnp.dot(hidden, w_out, preferred_element_type=jnp.float32)  8.32 us
    all_to_all x1, starting transfers between devices, per_device(): lax.all_to_all(payload[coarse_sender], 'lat', split_axis=0, concat_axis=0...  8.27 us
    gather x1, local copies, waits for them, and re-layouts, per_device(): grid_rows = grid_latent[g2m_sender]  5.97 us
    dot_general x2, matrix products, node_update(): jnp.dot(hidden, w_out, preferred_element_type=jnp.float32)  5.08 us
    dot_general x2, matrix products, node_update(): preact = jnp.dot(latent, w_in[:breadth], preferred_element_type=jnp.float32)  3.9 us
    dot_general x2, matrix products, sum_rows(): lax.dot_general(selector, message, (((0,), (0,)), ((), ())), preferred_el...  3.68 us
    dot_general x1, matrix products, per_device(): jnp.dot(edge_all, proc_edge_in[:breadth], preferred_element_type=jnp.floa...  3.3 us
  transfers between devices with their start and end apart: 5, of which 1 were waited for; matrix products, arithmetic and copies ran while one was open for 19% of the time, Pallas kernels for 0%

commit v1 on v0

v1 whole, which is shorter than its diff:
```python
import functools

import jax
import jax.numpy as jnp
from jax import lax
from jax.experimental import pallas as pl
from jax.experimental.pallas import tpu as pltpu
from jax.sharding import PartitionSpec as P

BR = 32
LANES = 128
CHUNK = 128
MESH = pl.DeviceIdType.MESH
F32 = jnp.float32
BF16 = jnp.bfloat16


def dot(a, b):
    return jnp.dot(a, b, preferred_element_type=F32)


def silu(x):
    half = 0.5 * x
    return half + half * jnp.tanh(half)


def normed(values, par):
    average = jnp.mean(values, axis=-1, keepdims=True)
    centred = values - average
    spread = jnp.mean(centred * centred, axis=-1, keepdims=True)
    return centred * lax.rsqrt(spread + 1e-05) * par[1:2, :] + par[2:3, :]


def mlp(preact, w_out, par):
    hidden = silu(preact + par[0:1, :]).astype(BF16)
    return normed(dot(hidden, w_out[...]), par)


def gather_matrix(row, extent):
    slots = row.shape[1]
    column = jnp.transpose(jnp.broadcast_to(row, (LANES, slots)))
    lane = lax.broadcasted_iota(jnp.int32, (slots, LANES), 1)
    pieces = [
        jnp.where(column == lane + start, 1.0, 0.0).astype(BF16)
        for start in range(0, extent, LANES)
    ]
    return pieces[0] if len(pieces) == 1 else jnp.concatenate(pieces, axis=1)


def sum_matrix(row, extent):
    slots = row.shape[1]
    node = lax.broadcasted_iota(jnp.int32, (extent, slots), 0)
    return jnp.where(node == row, 1.0, 0.0).astype(BF16)


NAMES = (
    "grid", "mesh", "g_edge", "g_send", "g_recv", "f_edge", "f_send", "f_recv", "c_edge", "c_send", "c_recv",
    "ee_in", "ee_out", "ee_par", "en_in", "en_out", "en_par",
    "pe_in", "pe_out", "pe_par", "pn_in", "pn_out", "pn_par",
)
ORDER = (
    "grid", "ee_in", "g_send", "g_edge", "mesh", "g_recv", "ee_par", "ee_out", "en_in", "f_edge", "pe_in",
    "c_edge", "f_send", "f_recv", "c_send", "c_recv", "en_par", "en_out", "pe_par", "pe_out",
    "pn_in", "pn_out", "pn_par",
)


def kernel(n, *refs):
    count = len(NAMES)
    sources = dict(zip(NAMES, refs[:count]))
    out_ref = refs[count]
    held = dict(zip(NAMES, refs[count + 1 : 2 * count + 1]))
    (
        g_table, r_table, leaving, arrived, r_terms, e_sum, acc, f_pre, c_pre, n_pre, enc, payload, proj,
        s_own, s_rim, s_recv, t_fine, s_far, s_crecv, t_far, rim, far_out, far_in,
        in_sem, halo_send, halo_recv, rim_send, rim_recv, far_send, far_recv,
    ) = refs[2 * count + 1 :]
    me = lax.axis_index("lat")
    reach = n // 2
    width = enc.shape[1]
    nodes = enc.shape[0]
    cap = leaving.shape[1]
    fine = f_pre.shape[0]
    far_rows = c_pre.shape[0]

    copies = {
        name: pltpu.make_async_copy(sources[name], held[name], in_sem.at[index])
        for index, name in enumerate(NAMES)
    }
    for name in ORDER:
        copies[name].start()

    rim[...] = jnp.zeros_like(rim)
    far_in[...] = jnp.zeros_like(far_in)

    @pl.when(me == n - 1)
    def _():
        arrived[0] = jnp.zeros((cap, width), BF16)

    @pl.when(me == 0)
    def _():
        arrived[1] = jnp.zeros((cap, width), BF16)

    barrier = pltpu.get_barrier_semaphore()

    def greet(step, carry):
        @pl.when(me - step >= 0)
        def _():
            pl.semaphore_signal(barrier, inc=1, device_id={"lat": me - step}, device_id_type=MESH)

        @pl.when(me + step < n)
        def _():
            pl.semaphore_signal(barrier, inc=1, device_id={"lat": me + step}, device_id_type=MESH)

        return carry

    lax.fori_loop(1, reach + 1, greet, 0)

    def halo(side, chunk):
        peer = me - 1 if side == 0 else me + 1
        rows = pl.ds(chunk * CHUNK, CHUNK)
        return pltpu.make_async_remote_copy(
            src_ref=leaving.at[side, rows],
            dst_ref=arrived.at[side, rows],
            send_sem=halo_send.at[side, chunk],
            recv_sem=halo_recv.at[side, chunk],
            device_id={"lat": peer},
            device_id_type=MESH,
        )

    def sends(side):
        return me > 0 if side == 0 else me < n - 1

    def receives(side):
        return me < n - 1 if side == 0 else me > 0

    chunks = cap // CHUNK

    copies["grid"].wait()
    copies["ee_in"].wait()
    w = held["ee_in"]
    g_table[...] = dot(held["grid"][...], w[width : 2 * width, :]).astype(BF16)
    copies["g_send"].wait()
    copies["g_edge"].wait()
    pl.semaphore_wait(barrier, jnp.minimum(me, reach) + jnp.minimum(n - 1 - me, reach))

    def edge_term(j, chunk):
        rows = slice(chunk * CHUNK, (chunk + 1) * CHUNK)
        chosen = gather_matrix(held["g_send"][j : j + 1, rows], nodes_grid)
        return (dot(held["g_edge"][j, rows, :], w[0:width, :]) + dot(chosen, g_table[...])).astype(BF16)

    nodes_grid = g_table.shape[0]
    for chunk in range(chunks):
        rows = slice(chunk * CHUNK, (chunk + 1) * CHUNK)
        for side in range(2):
            leaving[side, rows, :] = edge_term(2 * side, chunk)

            @pl.when(sends(side))
            def _():
                halo(side, chunk).start()

    copies["mesh"].wait()
    copies["g_recv"].wait()
    r_table[...] = dot(held["mesh"][...], w[2 * width :, :]).astype(BF16)
    copies["ee_par"].wait()
    copies["ee_out"].wait()
    e_par = held["ee_par"][...]
    for j in range(3):
        row = held["g_recv"][j : j + 1, :]
        r_terms[j] = dot(gather_matrix(row, nodes), r_table[...])
        e_sum[j] = sum_matrix(row, nodes)
    total = jnp.zeros((nodes, width), F32)
    for chunk in range(0, chunks, 2):
        rows = slice(chunk * CHUNK, (chunk + 2) * CHUNK)
        term = jnp.concatenate([edge_term(1, chunk), edge_term(1, chunk + 1)], axis=0)
        message = mlp(term.astype(F32) + r_terms[1, rows, :], held["ee_out"], e_par).astype(BF16)
        total = total + dot(e_sum[1, :, rows], message)
    acc[...] = total
    copies["en_in"].wait()
    n_pre[...] = dot(held["mesh"][...], held["en_in"][0:width, :])
    for name in ("f_edge", "pe_in", "c_edge", "f_send", "f_recv", "c_send", "c_recv"):
        copies[name].wait()
    pw = held["pe_in"]
    step = min(fine, 256)
    for start in range(0, fine, step):
        rows = slice(start, start + step)
        f_pre[rows, :] = dot(held["f_edge"][rows, :], pw[0:width, :])
        sender = held["f_send"][0:1, rows]
        s_own[rows, :] = gather_matrix(sender - BR, nodes)
        outer = jnp.where(sender < BR, sender, jnp.where(sender >= nodes + BR, sender - nodes, -1))
        s_rim[rows, :] = gather_matrix(outer, LANES)
        receiver = held["f_recv"][0:1, rows]
        s_recv[rows, :] = gather_matrix(receiver, nodes)
        t_fine[:, rows] = sum_matrix(receiver, nodes)
    far_step = min(far_rows, 256)
    for start in range(0, far_rows, far_step):
        rows = slice(start, start + far_step)
        c_pre[rows, :] = dot(held["c_edge"][rows, :], pw[0:width, :])
        s_far[rows, :] = gather_matrix(held["c_send"][0:1, rows], nodes)
        s_crecv[rows, :] = gather_matrix(held["c_recv"][0:1, rows], nodes)
        t_far[:, rows] = sum_matrix(held["c_recv"][0:1, rows], nodes)
    for name in ("en_par", "en_out", "pe_par", "pe_out", "pn_in", "pn_out", "pn_par"):
        copies[name].wait()

    for chunk in range(chunks):
        rows = slice(chunk * CHUNK, (chunk + 1) * CHUNK)
        for side in range(2):

            @pl.when(receives(side))
            def _():
                halo(side, chunk).wait_recv()

        z = jnp.concatenate(
            [arrived[side, rows, :].astype(F32) + r_terms[2 * side, rows, :] for side in range(2)], axis=0
        )
        message = mlp(z, held["ee_out"], e_par).astype(BF16)
        chosen = jnp.concatenate([e_sum[0, :, rows], e_sum[2, :, rows]], axis=1)
        acc[...] += dot(chosen, message)

    z = n_pre[...] + dot(acc[...].astype(BF16), held["en_in"][width:, :])
    enc[...] = (held["mesh"][...].astype(F32) + mlp(z, held["en_out"], held["en_par"][...])).astype(BF16)

    payload[...] = dot(enc[...], pw[width : 2 * width, :]).astype(BF16)

    def rim_copy(side):
        start = 0 if side == 0 else nodes - BR
        return pltpu.make_async_remote_copy(
            src_ref=payload.at[pl.ds(start, BR)],
            dst_ref=rim.at[pl.ds(BR if side == 0 else 0, BR)],
            send_sem=rim_send.at[side],
            recv_sem=rim_recv.at[side],
            device_id={"lat": me - 1 if side == 0 else me + 1},
            device_id_type=MESH,
        )

    for side in range(2):

        @pl.when(sends(side))
        def _():
            rim_copy(side).start()

    half = width // 2
    slots = far_rows // n
    for start in range(0, far_rows, far_step):
        rows = slice(start, start + far_step)
        picked = dot(s_far[rows, :], payload[...])
        low = picked[:, :half].reshape(far_step // slots, slots, half)
        high = picked[:, half:].reshape(far_step // slots, slots, half)
        far_out[start // slots : (start + far_step) // slots] = jnp.concatenate([low, high], axis=1).astype(BF16)

    def far_copy(slot_out, slot_in, peer):
        return pltpu.make_async_remote_copy(
            src_ref=far_out.at[slot_out],
            dst_ref=far_in.at[slot_in],
            send_sem=far_send.at[slot_out],
            recv_sem=far_recv.at[slot_in],
            device_id={"lat": peer},
            device_id_type=MESH,
        )

    def over_peers(act):
        def body(index, carry):
            distance = reach - index

            @pl.when(me - distance >= 0)
            def _():
                act(me - distance)

            @pl.when(me + distance < n)
            def _():
                act(me + distance)

            return carry

        lax.fori_loop(0, reach, body, 0)

    over_peers(lambda peer: far_copy(peer, me, peer).start())
    far_in[me] = far_out[me]

    proj[...] = dot(enc[...], pw[2 * width :, :]).astype(BF16)
    n_pre[...] = dot(enc[...], held["pn_in"][0:width, :])
    for start in range(0, fine, step):
        rows = slice(start, start + step)
        f_pre[rows, :] += dot(s_own[rows, :], payload[...]) + dot(s_recv[rows, :], proj[...])
    for start in range(0, far_rows, far_step):
        rows = slice(start, start + far_step)
        c_pre[rows, :] += dot(s_crecv[rows, :], proj[...])
    for side in range(2):

        @pl.when(receives(side))
        def _():
            rim_copy(side).wait_recv()

    p_par = held["pe_par"][...]
    total = jnp.zeros((nodes, width), F32)
    for start in range(0, fine, step):
        rows = slice(start, start + step)
        z = f_pre[rows, :] + dot(s_rim[rows, :], rim[...])
        message = mlp(z, held["pe_out"], p_par).astype(BF16)
        total = total + dot(t_fine[:, rows], message)
    over_peers(lambda peer: far_copy(peer, peer, peer).wait_recv())
    for start in range(0, far_rows, far_step):
        rows = slice(start, start + far_step)
        got = far_in[start // slots : (start + far_step) // slots].astype(F32)
        terms = jnp.concatenate(
            [got[:, :slots, :].reshape(far_step, half), got[:, slots:, :].reshape(far_step, half)], axis=1
        )
        message = mlp(c_pre[rows, :] + terms, held["pe_out"], p_par).astype(BF16)
        total = total + dot(t_far[:, rows], message)
    z = n_pre[...] + dot(total.astype(BF16), held["pn_in"][width:, :])
    out_ref[...] = (enc[...].astype(F32) + mlp(z, held["pn_out"], held["pn_par"][...])).astype(BF16)

    for side in range(2):

        @pl.when(sends(side))
        def _():
            for chunk in range(chunks):
                halo(side, chunk).wait_send()
            rim_copy(side).wait_send()

    over_peers(lambda peer: far_copy(peer, me, peer).wait_send())


def per_device(n, *args):
    args = list(args)
    width = args[0].shape[1]
    for index in (6, 7, 9, 10):
        args[index] = args[index].reshape(1, -1)
    args[8] = args[8].reshape(-1, width)
    grid_nodes, nodes, cap = args[0].shape[0], args[1].shape[0], args[2].shape[1]
    fine, far = args[5].shape[0], args[8].shape[0]
    slots = far // n
    chunks = cap // CHUNK
    vmem = pltpu.VMEM
    dma = pltpu.SemaphoreType.DMA
    scratch = [vmem(a.shape, a.dtype) for a in args] + [
        vmem((grid_nodes, width), BF16),
        vmem((nodes, width), BF16),
        vmem((2, cap, width), BF16),
        vmem((2, cap, width), BF16),
        vmem((3, cap, width), F32),
        vmem((3, nodes, cap), BF16),
        vmem((nodes, width), F32),
        vmem((fine, width), F32),
        vmem((far, width), F32),
        vmem((nodes, width), F32),
        vmem((nodes, width), BF16),
        vmem((nodes, width), BF16),
        vmem((nodes, width), BF16),
        vmem((fine, nodes), BF16),
        vmem((fine, LANES), BF16),
        vmem((fine, nodes), BF16),
        vmem((nodes, fine), BF16),
        vmem((far, nodes), BF16),
        vmem((far, nodes), BF16),
        vmem((nodes, far), BF16),
        vmem((LANES, width), BF16),
        vmem((n, 2 * slots, width // 2), BF16),
        vmem((n, 2 * slots, width // 2), BF16),
        dma((len(args),)),
        dma((2, chunks)),
        dma((2, chunks)),
        dma((2,)),
        dma((2,)),
        dma((n,)),
        dma((n,)),
    ]
    return pl.pallas_call(
        functools.partial(kernel, n),
        out_shape=jax.ShapeDtypeStruct((nodes, width), BF16),
        in_specs=[pl.BlockSpec(memory_space=pl.ANY)] * len(args),
        out_specs=pl.BlockSpec(memory_space=vmem),
        scratch_shapes=scratch,
        compiler_params=pltpu.CompilerParams(
            collective_id=0, has_side_effects=True, vmem_limit_bytes=56 * 1024 * 1024
        ),
        cost_estimate=pl.CostEstimate(flops=10**10, bytes_accessed=12 * 10**6, transcendentals=2 * 10**6),
    )(*args)


def solution(mesh):
    in_specs = (
        P(("groups", "lat"), None),
        P(("groups", "lat"), None),
        P("lat", None, None),
        P("lat", None),
        P("lat", None),
        P("lat", None),
        P("lat"),
        P("lat"),
        P("lat", None, None),
        P("lat", None),
        P("lat", None),
    ) + (P(),) * 12
    return jax.shard_map(
        functools.partial(per_device, mesh.shape["lat"]),
        mesh=mesh,
        in_specs=in_specs,
        out_specs=P(("groups", "lat"), None),
        check_vma=False,
    )
```

time: 90.8 us -> 33.5 us (0.37)
  the two profiles are of different devices: /device:TPU:0 before, /device:TPU:1 now
where the time goes in v1:
time: 33.5 us; the launch traced here: 33.3 us
  Pallas kernels  28.6 us (85%)
  local copies, waits for them, and re-layouts  4.67 us (14%)
    pallas_call x1, Pallas kernels, per_device(): pl.pallas_call(functools.partial(kernel, n), out_shape=jax.ShapeDtypeStru...  28.6 us
    unnamed x3, local copies, waits for them, and re-layouts  3.38 us
    reshape x2, local copies, waits for them, and re-layouts, per_device(): args[index] = args[index].reshape(1, -1)  1.29 us

profile of v1, /device:TPU:1, one launch (start us, length us, event | category | flops | bytes accessed | tf_op | source)
XLA Modules:
  0.0 33.3 jit_solution(15154256925256273853)
XLA Ops:
  0.0 0.8 %copy.26 = s32[16,8]{1,0:T(8,128)S(1)} copy(s32[16,8]{0,1:T(8,128)} %param.32) | data formatting | bytes 1024 | tf_op args[9]
  0.8 0.6 %reshape.18.refs_9_ = s32[1,128]{1,0:T(1,128)} reshape(s32[16,8]{1,0:T(8,128)S(1)} %copy.26) | data formatting | bytes 1024 | tf_op jit(solution)/shard_map/reshape | solution.py:328
  1.4 0.8 %copy.27 = s32[16,8]{1,0:T(8,128)S(1)} copy(s32[16,8]{0,1:T(8,128)} %param.33) | data formatting | bytes 1024 | tf_op args[10]
  2.1 0.7 %reshape.19.refs_10_ = s32[1,128]{1,0:T(1,128)} reshape(s32[16,8]{1,0:T(8,128)S(1)} %copy.27) | data formatting | bytes 1024 | tf_op jit(solution)/shard_map/reshape | solution.py:328
  2.8 28.6 %shard_map.217 = bf16[512,512]{1,0:T(8,128)(2,1)} custom-call(bf16[512,512]{1,0:T(8,128)(2,1)} %refs_0_.1, bf16[512,512]{1,0:T(8,128)(2,1)} %refs_1_.1, bf16[3,512,512]{2,1,0:T(8,128)(2,1)} %refs_2_.1, s32[3,512]{1,0:T(4,128)} %refs_3_.1, s32[3,512]{1,0:T(4,128)} %refs_4_.1, bf16[1024,512]{1,0:T(8,128)(2,1)} %refs_5_.1, s32[1,1024]{1,0:T(1,128)} %bitcast.4, ...), custom_call_target="tpu_custom_call" | custom-call | flops 10000000000 | bytes 12000000 | tf_op jit(solution)/shard_map/pallas_call | solution.py:368
  31.4 1.9 %copy.29 = bf16[512,512]{1,0:T(8,128)(2,1)} copy(bf16[512,512]{1,0:T(8,128)(2,1)} %shard_map.217) | data formatting | bytes 1048576
